TPU v7x, 512 devices: a whole 4x4x16 slice. The times are simulated.
512 devices in a mesh: space: 32 (over z, core), tm: 16 (over x, y).
Axes of the slice: x: 4, y: 4, z: 16, core: 2. Of those that a mesh axis runs over, the one named last changes fastest.
Arguments:
- recordings: bfloat16 [2, 3, 512, 32768], P(None, None, 'space', 'tm'), may hold values from -30 to 30
- owner: int32 [512, 1], P('space'), may hold values from 0 to 31; in each aligned block of 16 rows (0 to 15, 16 to 31, ...) at most 2 rows name the same one
- valid_range: int32 [512, 2], P('space'), may hold values from 0 to 32768, as said below
- bin_mask: int32 [512, 96], P('space'), may hold values 0 or 1
Outputs:
- adjoint: bfloat16 [3, 2048, 32768], P(None, 'space', 'tm')
Inputs may be any that keep to these rules, and one draw needn't show every extreme that they name: `owner`: among the 16 receivers listed on one index of space, no subdomain owns more than 2; some subdomain owns exactly 2 of them. `valid_range`: column 0 is below column 1 in every row.
All inputs are finite; a program needn't handle non-finite values. No bound on the sum of `bin_mask` on one device may be relied on, other than what follows from the above.
Results may differ from a plain program's by a relative error of at most 0.013.
Values may be sent and summed in bfloat16 or wider, within the bound.
A program may use at most 128 MiB of HBM per device.

v0:
```python
import math

import jax
import jax.numpy as jnp
from jax import lax
from jax.sharding import PartitionSpec as P

BINS = 96
HOP = 256
HALO = 1024
KERNEL = 2304


WATER = 0.1
EPSILON = 1e-06


def with_halo(block, sides, width):
    for axis, dim in sides:
        count = lax.axis_size(axis)
        forward = [(i, i + 1) for i in range(count - 1)]
        backward = [(target, source) for source, target in forward]
        low = lax.ppermute(
            lax.slice_in_dim(block, block.shape[dim] - width, None, axis=dim), axis, forward
        )
        high = lax.ppermute(lax.slice_in_dim(block, 0, width, axis=dim), axis, backward)
        block = jnp.concatenate([low, block, high], axis=dim)
    return block


def shifted(block, axis, distance):
    devices = range(lax.axis_size(axis))
    route = [(i - distance, i) for i in devices if i - distance in devices]
    return lax.ppermute(block, axis, route)


def cq_kernel(kern_len, bins):
    octave_bins = bins // 8
    index = jnp.arange(bins).astype(jnp.float32)
    freq = 0.25 * jnp.exp2((index - (bins - 1)) / octave_bins)
    quality = 1.0 / (2.0 ** (1.0 / octave_bins) - 1.0)
    support = jnp.minimum(quality / freq, float(kern_len))
    offset = jnp.arange(kern_len).astype(jnp.float32) - 0.5 * (kern_len - 1)
    ratio = offset[:, None] / support[None, :]
    window = jnp.where(jnp.abs(ratio) < 0.5, 0.5 + 0.5 * jnp.cos(2.0 * math.pi * ratio), 0.0)
    window = window / jnp.sqrt(jnp.sum(window * window, axis=0, keepdims=True))
    cycles = offset[:, None] * freq[None, :]
    phase = cycles - jnp.floor(cycles)
    table = jnp.concatenate(
        [window * jnp.cos(2.0 * math.pi * phase), -window * jnp.sin(2.0 * math.pi * phase)], axis=1
    )
    return table.astype(jnp.bfloat16)


def adjoint_of(syn_re, syn_im, obs_re, obs_im, weight):
    level = (
        WATER * jnp.mean(obs_re * obs_re + obs_im * obs_im, axis=(-2, -1), keepdims=True) + EPSILON
    )
    syn_norm = jnp.sqrt(syn_re * syn_re + syn_im * syn_im + level)
    obs_norm = jnp.sqrt(obs_re * obs_re + obs_im * obs_im + level)
    diff_re = weight * (syn_re / syn_norm - obs_re / obs_norm)
    diff_im = weight * (syn_im / syn_norm - obs_im / obs_norm)
    inner = (syn_re * diff_re + syn_im * diff_im) / (syn_norm * syn_norm * syn_norm)
    return (diff_re / syn_norm - syn_re * inner, diff_im / syn_norm - syn_im * inner)


def analyse(blocks, table, frames):
    taps = table.shape[0] // HOP
    unfolded = jnp.concatenate([blocks[..., tap : tap + frames, :] for tap in range(taps)], axis=-1)
    return jnp.einsum("...fh,hk->...fk", unfolded, table, preferred_element_type=jnp.float32)


def synthesise(coefs, table, frames):
    taps = table.shape[0] // HOP
    term = jnp.einsum("...fk,hk->...fh", coefs, table, preferred_element_type=jnp.float32)
    term = term.reshape(term.shape[:-1] + (taps, HOP))
    lead = len(term.shape) - 3
    ext = jnp.zeros(coefs.shape[:-2] + (frames + taps - 1, HOP), jnp.float32)
    for tap in range(taps):
        widths = [(0, 0)] * lead + [(tap, taps - 1 - tap), (0, 0)]
        ext = ext + jnp.pad(term[..., tap, :], widths)
    return ext


def frame_weight(ranges, masks, frames_all):
    centers = jnp.arange(frames_all, dtype=jnp.int32) * HOP + HOP // 2
    inside = (ranges[:, 0:1] <= centers[None, :]) & (centers[None, :] < ranges[:, 1:2])
    return inside.astype(jnp.float32)[:, :, None] * masks.astype(jnp.float32)[:, None, :]


def misfit(coefs, weight):
    adj_re, adj_im = adjoint_of(
        coefs[0, ..., :BINS],
        coefs[0, ..., BINS:],
        coefs[1, ..., :BINS],
        coefs[1, ..., BINS:],
        weight,
    )
    joined = jnp.concatenate([adj_re, adj_im], axis=-1)
    return joined.reshape(joined.shape[:2] + (joined.shape[2] * joined.shape[3],)).astype(
        jnp.bfloat16
    )


def on_device(recordings, owner, valid_range, bin_mask):
    table = cq_kernel(KERNEL, BINS)
    margin = HALO // HOP
    width = 2 * BINS
    groups = lax.axis_size("tm")
    comps = recordings.shape[1]
    rec_dev = recordings.shape[2]
    samples_dev = recordings.shape[3]
    frames_dev = samples_dev // HOP
    rec_group = rec_dev // groups
    first_row = lax.axis_index("tm") * rec_group
    ranges = lax.dynamic_slice_in_dim(valid_range, first_row, rec_group, 0)
    masks = lax.dynamic_slice_in_dim(bin_mask, first_row, rec_group, 0)
    extended = with_halo(recordings, (("tm", 3),), HALO)
    blocks = extended.reshape(2, comps, rec_dev, frames_dev + 2 * margin, HOP)
    coefs = analyse(blocks, table, frames_dev)
    packed = coefs.astype(jnp.bfloat16).reshape(2, comps, rec_dev, frames_dev * width)
    weight = frame_weight(ranges, masks, frames_dev * groups)
    pieces = lax.all_to_all(packed, "tm", split_axis=2, concat_axis=3, tiled=True)
    items = pieces.shape[1]
    frames_all = pieces.shape[3] // width
    local_coefs = pieces.astype(jnp.float32).reshape(2, items, rec_group, frames_all, width)
    adjoint_local = misfit(local_coefs, weight)
    adjoint_back = lax.all_to_all(adjoint_local, "tm", split_axis=2, concat_axis=1, tiled=True)
    adjoint_frames = adjoint_back.reshape(comps, rec_dev, frames_dev, width)
    ext = synthesise(adjoint_frames, table, frames_dev)
    flat = ext.reshape(comps, rec_dev, (frames_dev + 2 * margin) * HOP)
    middle = flat[:, :, HALO : HALO + samples_dev]
    from_before = shifted(flat[:, :, HALO + samples_dev :].astype(jnp.bfloat16), "tm", 1).astype(
        jnp.float32
    )
    from_after = shifted(flat[:, :, :HALO].astype(jnp.bfloat16), "tm", -1).astype(jnp.float32)
    middle = middle.at[:, :, :HALO].add(from_before)
    middle = middle.at[:, :, samples_dev - HALO :].add(from_after)
    series = middle.astype(jnp.bfloat16)
    count = lax.axis_size("space")
    most = max(2, 3 * rec_dev // (2 * count))
    target = owner[:, 0]
    onehot = (target[:, None] == jnp.arange(count, dtype=jnp.int32)[None, :]).astype(jnp.int32)
    before = jnp.cumsum(onehot, axis=0) - onehot
    rank = jnp.sum(before * onehot, axis=1)
    slot = target * most + rank
    select = (jnp.arange(count * most, dtype=jnp.int32)[:, None] == slot[None, :]).astype(
        jnp.bfloat16
    )
    outgoing = jnp.einsum("sr,crt->cst", select, series, preferred_element_type=jnp.float32).astype(
        jnp.bfloat16
    )
    return lax.all_to_all(outgoing, "space", split_axis=1, concat_axis=1, tiled=True)


def solution(mesh):
    return jax.shard_map(
        on_device,
        mesh=mesh,
        in_specs=(
            P(None, None, "space", "tm"),
            P("space", None),
            P("space", None),
            P("space", None),
        ),
        out_specs=P(None, "space", "tm"),
        check_vma=False,
    )
```

profile of v0, /device:TPU:1, one launch (start us, length us, event | category | flops | bytes accessed | tf_op | source)
XLA Modules:
  0.0 346.1 jit_solution(11848009665123763137)
XLA Ops:
  0.0 1.1 fusion.24
  1.1 4.0 %collective-permute-start = (bf16[2,3,16,1024]{3,2,1,0:T(8,128)(2,1)S(1)}, bf16[2,3,16,1024]{3,2,1,0:T(8,128)(2,1)S(1)}, u32[]{:S(2)}, u32[]{:S(2)}) collective-permute-start(bf16[2,3,16,1024]{3,2,1,0:T(8,128)(2,1)S(1)} %get-tuple-element.42), channel_id=1, source_target_pairs={{0,1},{1,2},{2,3},{3,4},{4,5},{5,6},{6,7},{7,8},{8,9},{9,10},{10,1... | collective-permute-start | bytes 589832 | tf_op jit(solution)/shard_map/ppermute | solution.py:23
  5.2 1.3 collective-permute-start.1
  6.5 3.4 multiply_reduce_fusion
  10.0 6.7 %multiply_convert_fusion.3 = (bf16[2304,96]{0,1:T(8,128)(2,1)S(1)}, bf16[2304,96]{0,1:T(8,128)(2,1)S(1)}) fusion(f32[96]{0:T(128)S(1)} %get-tuple-element.51, f32[2304]{0:T(1024)S(1)} %convert_add_fusion.1, f32[96]{0:T(128)S(1)} %sqrt.38, f32[96]{0:T(128)S(1)} %get-tuple-element.50), kind=kLoop, calls=%fused_computation.19 | loop fusion | flops 3760128 | bytes 895104 | tf_op jit(solution)/shard_map/convert.7
  16.6 6.8 %multiply_convert_fusion.1 = (bf16[9,256,96]{1,2,0:T(8,128)(2,1)S(1)}, bf16[9,256,96]{1,2,0:T(8,128)(2,1)S(1)}) fusion(f32[96]{0:T(128)S(1)} %get-tuple-element.51, f32[9,256]{1,0:T(8,128)S(1)} %convert_add_fusion, f32[96]{0:T(128)S(1)} %sqrt.38, f32[96]{0:T(128)S(1)} %get-tuple-element.50), kind=kLoop, calls=%fused_computation.15 | loop fusion | flops 3760128 | bytes 895104 | tf_op jit(solution)/shard_map/convert.3
  23.6 0.7 fusion.19
  26.0 1.1 convolution_convert_fusion.1
  27.4 1.0 copy.61
  28.4 7.5 %all-to-all-start = ((bf16[2,3,16,1536]{3,0,1,2:T(2,128)(2,1)}), bf16[2,3,16,1536]{3,0,1,2:T(2,128)(2,1)S(1)}, u32[]{:S(2)}, u32[]{:S(2)}) async-start(bf16[2,3,16,1536]{3,0,1,2:T(2,128)(2,1)} %copy.61), calls=%async_computation | async-start | bytes 589824 | tf_op jit(solution)/shard_map/all_to_all | solution.py:123
  36.0 1.2 and_convert_fusion
  37.3 6.3 %all-to-all-done = bf16[2,3,16,1536]{3,0,1,2:T(2,128)(2,1)S(1)} async-done(((bf16[2,3,16,1536]{3,0,1,2:T(2,128)(2,1)}), bf16[2,3,16,1536]{3,0,1,2:T(2,128)(2,1)S(1)}, u32[]{:S(2)}, u32[]{:S(2)}) %all-to-all-start) | async-done | bytes 294944 | tf_op jit(solution)/shard_map/all_to_all | solution.py:123
  44.8 19.4 %copy.66 = bf16[3,1,24576]{0,1,2:T(2,128)(2,1)} copy(bf16[3,1,24576]{2,0,1:T(4,128)(2,1)S(1)} %convert_element_type.135) | data formatting | bytes 294912 | tf_op jit(solution)/shard_map/convert_element_type | solution.py:100
  64.8 134.9 %reduce.5 = bf16[24576,3]{1,0:T(8,128)(2,1)} reduce(bf16[24576,1,3]{2,1,0:T(2,128)(2,1)} %bitcast.152, bf16[]{:T(256)} %broadcast.341), dimensions={1}, to_apply=%bitcast.148.reduce_sub_computation | reduce | bytes 294914
  199.7 10.0 %reshape.529 = bf16[16,2,2304]{2,1,0:T(2,128)(2,1)} reshape(bf16[24576,3]{1,0:T(8,128)(2,1)} %reduce.5) | data formatting | bytes 294912
  209.7 3.8 %all-to-all-start.1 = ((bf16[16,2,2304]{2,1,0:T(2,128)(2,1)}), bf16[16,2,2304]{2,1,0:T(2,128)(2,1)S(1)}, u32[]{:S(2)}, u32[]{:S(2)}) async-start(bf16[16,2,2304]{2,1,0:T(2,128)(2,1)} %reshape.529), calls=%async_computation.1 | async-start | bytes 294912 | tf_op jit(solution)/shard_map/all_to_all | solution.py:128
  213.8 6.3 %all-to-all-done.1 = bf16[16,2,2304]{2,1,0:T(2,128)(2,1)S(1)} async-done(((bf16[16,2,2304]{2,1,0:T(2,128)(2,1)}), bf16[16,2,2304]{2,1,0:T(2,128)(2,1)S(1)}, u32[]{:S(2)}, u32[]{:S(2)}) %all-to-all-start.1) | async-done | bytes 147488 | tf_op jit(solution)/shard_map/all_to_all | solution.py:128
  220.1 14.4 %reshape.530 = bf16[24576,1,3]{2,1,0:T(2,128)(2,1)} reshape(bf16[16,2,2304]{2,1,0:T(2,128)(2,1)S(1)} %all-to-all-done.1) | data formatting | bytes 294912
  234.5 23.3 %copy.67 = bf16[3,1,24576]{2,0,1:T(4,128)(2,1)S(1)} copy(bf16[3,1,24576]{0,1,2:T(2,128)(2,1)} %bitcast.151) | data formatting | bytes 294912 | tf_op jit(solution)/shard_map/all_to_all | solution.py:128
  259.9 2.1 collective-permute-start.2
  262.0 1.3 collective-permute-start.3
  263.6 3.8 %collective-permute-done.3 = bf16[3,16,1024]{2,1,0:T(8,128)(2,1)S(1)} collective-permute-done((bf16[3,16,1024]{2,1,0:T(8,128)(2,1)S(1)}, bf16[3,16,1024]{2,1,0:T(8,128)(2,1)S(1)}, u32[]{:S(2)}, u32[]{:S(2)}) %collective-permute-start.3) | collective-permute-done | bytes 98336 | tf_op jit(solution)/shard_map/ppermute | solution.py:34
  268.6 76.0 %all_to_all.23 = bf16[3,64,2048]{2,0,1:T(4,128)(2,1)S(1)} all-to-all(bf16[3,64,2048]{2,0,1:T(4,128)(2,1)S(1)} %copy.76), channel_id=1, replica_groups=mesh['space'=32,'tm'=16] {'space'}, dimensions={1} | all-to-all | bytes 1572864 | tf_op jit(solution)/shard_map/all_to_all | solution.py:153
  344.6 1.5 copy.77
  (52 shorter events, 7.8 us)
Async XLA Ops:
  0.0 23.5 %copy-start = (s32[16,2]{0,1:T(2,128)S(1)}, s32[16,2]{0,1:T(2,128)}, u32[]{:S(2)}) copy-start(s32[16,2]{0,1:T(2,128)} %param.10) | copy-start | bytes 388
  0.0 24.8 %copy-start.1 = (bf16[2,3,16,2048]{3,2,1,0:T(8,128)(2,1)S(1)}, bf16[2,3,16,2048]{3,2,1,0:T(8,128)(2,1)}, u32[]{:S(2)}) copy-start(bf16[2,3,16,2048]{3,2,1,0:T(8,128)(2,1)} %param.8) | copy-start | bytes 1179652
  1.1 23.7 %collective-permute-start = (bf16[2,3,16,1024]{3,2,1,0:T(8,128)(2,1)S(1)}, bf16[2,3,16,1024]{3,2,1,0:T(8,128)(2,1)S(1)}, u32[]{:S(2)}, u32[]{:S(2)}) collective-permute-start(bf16[2,3,16,1024]{3,2,1,0:T(8,128)(2,1)S(1)} %get-tuple-element.42), channel_id=1, source_target_pairs={{0,1},{1,2},{2,3},{3,4},{4,5},{5,6},{6,7},{7,8},{8,9},{9,10},{10,1... | collective-permute-start | bytes 589832 | tf_op jit(solution)/shard_map/ppermute | solution.py:23
  5.2 19.6 %collective-permute-start.1 = (bf16[2,3,16,1024]{3,2,1,0:T(8,128)(2,1)S(1)}, bf16[2,3,16,1024]{3,2,1,0:T(8,128)(2,1)S(1)}, u32[]{:S(2)}, u32[]{:S(2)}) collective-permute-start(bf16[2,3,16,1024]{3,2,1,0:T(8,128)(2,1)S(1)} %get-tuple-element.43), channel_id=1, source_target_pairs={{1,0},{2,1},{3,2},{4,3},{5,4},{6,5},{7,6},{8,7},{9,8},{10,9},{11,1... | collective-permute-start | bytes 589832 | tf_op jit(solution)/shard_map/ppermute | solution.py:26
  28.4 15.1 %all-to-all-start = ((bf16[2,3,16,1536]{3,0,1,2:T(2,128)(2,1)}), bf16[2,3,16,1536]{3,0,1,2:T(2,128)(2,1)S(1)}, u32[]{:S(2)}, u32[]{:S(2)}) async-start(bf16[2,3,16,1536]{3,0,1,2:T(2,128)(2,1)} %copy.61), calls=%async_computation | async-start | bytes 589824 | tf_op jit(solution)/shard_map/all_to_all | solution.py:123
  199.7 13.8 %copy-start.2 = (s32[16,1]{0,1:T(1,128)S(1)}, s32[16,1]{0,1:T(1,128)}, u32[]{:S(2)}) copy-start(s32[16,1]{0,1:T(1,128)} %param.9) | copy-start | bytes 196
  209.7 10.4 %all-to-all-start.1 = ((bf16[16,2,2304]{2,1,0:T(2,128)(2,1)}), bf16[16,2,2304]{2,1,0:T(2,128)(2,1)S(1)}, u32[]{:S(2)}, u32[]{:S(2)}) async-start(bf16[16,2,2304]{2,1,0:T(2,128)(2,1)} %reshape.529), calls=%async_computation.1 | async-start | bytes 294912 | tf_op jit(solution)/shard_map/all_to_all | solution.py:128
  259.9 3.7 %collective-permute-start.2 = (bf16[3,16,1024]{2,1,0:T(8,128)(2,1)S(1)}, bf16[3,16,1024]{2,1,0:T(8,128)(2,1)S(1)}, u32[]{:S(2)}, u32[]{:S(2)}) collective-permute-start(bf16[3,16,1024]{2,1,0:T(8,128)(2,1)S(1)} %get-tuple-element.41), channel_id=1, source_target_pairs={{0,1},{1,2},{2,3},{3,4},{4,5},{5,6},{6,7},{7,8},{8,9},{9,10},{10,1... | collective-permute-start | bytes 294920 | tf_op jit(solution)/shard_map/ppermute | solution.py:34
  262.0 5.4 %collective-permute-start.3 = (bf16[3,16,1024]{2,1,0:T(8,128)(2,1)S(1)}, bf16[3,16,1024]{2,1,0:T(8,128)(2,1)S(1)}, u32[]{:S(2)}, u32[]{:S(2)}) collective-permute-start(bf16[3,16,1024]{2,1,0:T(8,128)(2,1)S(1)} %get-tuple-element.40), channel_id=1, source_target_pairs={{1,0},{2,1},{3,2},{4,3},{5,4},{6,5},{7,6},{8,7},{9,8},{10,9},{11,1... | collective-permute-start | bytes 294920 | tf_op jit(solution)/shard_map/ppermute | solution.py:34
where the time goes:
time: 348 us; the launch traced here: 346 us
  other arithmetic  156 us (45%)
  blocking collectives  76 us (22%)
  local copies, waits for them, and re-layouts  75.2 us (22%)
  starting transfers between devices  20 us (6%)
  waiting for transfers between devices  16.6 us (5%)
    unnamed x1, other arithmetic  135 us
    all_to_all x1, blocking collectives, on_device(): lax.all_to_all(outgoing, 'space', split_axis=1, concat_axis=1, tiled=True)  76 us
    unnamed x18, local copies, waits for them, and re-layouts  26 us
    all_to_all x1, local copies, waits for them, and re-layouts, on_device(): lax.all_to_all(adjoint_local, 'tm', split_axis=2, concat_axis=1, tiled=True)  23.3 us
    convert_element_type x2, local copies, waits for them, and re-layouts, misfit(): joined.reshape(joined.shape[:2] + (joined.shape[2] * joined.shape[3],))  19.7 us
    another operation x4, other arithmetic  13.9 us
    all_to_all x1, starting transfers between devices, on_device(): lax.all_to_all(packed, 'tm', split_axis=2, concat_axis=3, tiled=True)  7.54 us
  transfers between devices with their start and end apart: 6, of which 4 were waited for; matrix products, arithmetic and copies ran while one was open for 6% of the time, Pallas kernels for 0%

commit v1 on v0

--- a/solution.py
+++ b/solution.py
@@ -140,9 +140,9 @@
     count = lax.axis_size("space")
     most = max(2, 3 * rec_dev // (2 * count))
     target = owner[:, 0]
-    onehot = (target[:, None] == jnp.arange(count, dtype=jnp.int32)[None, :]).astype(jnp.int32)
-    before = jnp.cumsum(onehot, axis=0) - onehot
-    rank = jnp.sum(before * onehot, axis=1)
+    place = jnp.arange(rec_dev, dtype=jnp.int32)
+    earlier = (target[:, None] == target[None, :]) & (place[None, :] < place[:, None])
+    rank = jnp.sum(earlier.astype(jnp.int32), axis=1)
     slot = target * most + rank
     select = (jnp.arange(count * most, dtype=jnp.int32)[:, None] == slot[None, :]).astype(
         jnp.bfloat16

time: 348 us -> 343 us (0.986)
  waiting for transfers between devices: 16.6 us -> 10.2 us
    all_to_all x1, waiting for transfers between devices: 6.3 us -> 0.01 us  [on_device(): lax.all_to_all(adjoint_local, 'tm', split_axis=2, concat_axis=1, tiled=True)]
    unnamed x18 -> x16, local copies, waits for them, and re-layouts: 26 us -> 26 us
    another operation x5 -> x4, other arithmetic: 14 us -> 13.9 us
  transfers between devices with their start and end apart: 6 -> 6, of which waited for: 4 -> 3; matrix products, arithmetic and copies ran while one was open for 6% -> 6% of each run, Pallas kernels for 0% -> 0%
where the time goes in v1:
time: 343 us; the launch traced here: 341 us
  other arithmetic  157 us (46%)
  local copies, waits for them, and re-layouts  75.3 us (22%)
  blocking collectives  75.1 us (22%)
  starting transfers between devices  21.1 us (6%)
  waiting for transfers between devices  10.2 us (3%)
    unnamed x1, other arithmetic  135 us
    all_to_all x1, blocking collectives, on_device(): lax.all_to_all(outgoing, 'space', split_axis=1, concat_axis=1, tiled=True)  75.1 us
    unnamed x16, local copies, waits for them, and re-layouts  26 us
    all_to_all x1, local copies, waits for them, and re-layouts, on_device(): lax.all_to_all(adjoint_local, 'tm', split_axis=2, concat_axis=1, tiled=True)  23.3 us
    convert_element_type x2, local copies, waits for them, and re-layouts, misfit(): joined.reshape(joined.shape[:2] + (joined.shape[2] * joined.shape[3],))  19.7 us
    another operation x4, other arithmetic  13.9 us
    all_to_all x1, starting transfers between devices, on_device(): lax.all_to_all(packed, 'tm', split_axis=2, concat_axis=3, tiled=True)  7.54 us
  transfers between devices with their start and end apart: 6, of which 3 were waited for; matrix products, arithmetic and copies ran while one was open for 6% of the time, Pallas kernels for 0%

profile of v1, /device:TPU:1, one launch (start us, length us, event | category | flops | bytes accessed | tf_op | source)
XLA Modules:
  0.0 340.9 jit_solution(2724905111548227926)
XLA Ops:
  0.0 1.1 fusion.24
  1.1 4.0 %collective-permute-start = (bf16[2,3,16,1024]{3,2,1,0:T(8,128)(2,1)S(1)}, bf16[2,3,16,1024]{3,2,1,0:T(8,128)(2,1)S(1)}, u32[]{:S(2)}, u32[]{:S(2)}) collective-permute-start(bf16[2,3,16,1024]{3,2,1,0:T(8,128)(2,1)S(1)} %get-tuple-element.42), channel_id=1, source_target_pairs={{0,1},{1,2},{2,3},{3,4},{4,5},{5,6},{6,7},{7,8},{8,9},{9,10},{10,1... | collective-permute-start | bytes 589832 | tf_op jit(solution)/shard_map/ppermute | solution.py:23
  5.1 1.3 collective-permute-start.1
  6.5 3.4 %multiply_reduce_fusion = f32[96]{0:T(128)S(1)} fusion(f32[96]{0:T(128)S(1)} %get-tuple-element.50, f32[2304]{0:T(1024)S(1)} %convert_add_fusion.1), kind=kLoop, calls=%fused_computation.20 | loop fusion | flops 1990560 | bytes 9984 | tf_op jit(solution)/shard_map/reduce_sum | solution.py:46
  10.6 6.6 %multiply_convert_fusion.3 = (bf16[2304,96]{0,1:T(8,128)(2,1)S(1)}, bf16[2304,96]{0,1:T(8,128)(2,1)S(1)}) fusion(f32[96]{0:T(128)S(1)} %get-tuple-element.51, f32[2304]{0:T(1024)S(1)} %convert_add_fusion.1, f32[96]{0:T(128)S(1)} %sqrt.38, f32[96]{0:T(128)S(1)} %get-tuple-element.50), kind=kLoop, calls=%fused_computation.19 | loop fusion | flops 3760128 | bytes 895104 | tf_op jit(solution)/shard_map/convert.7
  17.2 0.7 fusion.19
  18.0 1.1 pad_maximum_fusion
  20.2 1.1 convolution_convert_fusion.1
  21.6 1.0 copy.78
  22.6 7.5 %all-to-all-start = ((bf16[2,3,16,1536]{3,0,1,2:T(2,128)(2,1)}), bf16[2,3,16,1536]{3,0,1,2:T(2,128)(2,1)S(1)}, u32[]{:S(2)}, u32[]{:S(2)}) async-start(bf16[2,3,16,1536]{3,0,1,2:T(2,128)(2,1)} %copy.78), calls=%async_computation | async-start | bytes 589824 | tf_op jit(solution)/shard_map/all_to_all | solution.py:123
  30.2 1.3 and_convert_fusion
  31.5 6.2 %all-to-all-done = bf16[2,3,16,1536]{3,0,1,2:T(2,128)(2,1)S(1)} async-done(((bf16[2,3,16,1536]{3,0,1,2:T(2,128)(2,1)}), bf16[2,3,16,1536]{3,0,1,2:T(2,128)(2,1)S(1)}, u32[]{:S(2)}, u32[]{:S(2)}) %all-to-all-start) | async-done | bytes 294944 | tf_op jit(solution)/shard_map/all_to_all | solution.py:123
  39.0 19.4 %copy.83 = bf16[3,1,24576]{0,1,2:T(2,128)(2,1)} copy(bf16[3,1,24576]{2,0,1:T(4,128)(2,1)S(1)} %convert_element_type.135) | data formatting | bytes 294912 | tf_op jit(solution)/shard_map/convert_element_type | solution.py:100
  58.9 135.0 %reduce.5 = bf16[24576,3]{1,0:T(8,128)(2,1)} reduce(bf16[24576,1,3]{2,1,0:T(2,128)(2,1)} %bitcast.152, bf16[]{:T(256)} %broadcast.336), dimensions={1}, to_apply=%bitcast.148.reduce_sub_computation | reduce | bytes 294914
  193.9 10.0 %reshape.530 = bf16[16,2,2304]{2,1,0:T(2,128)(2,1)} reshape(bf16[24576,3]{1,0:T(8,128)(2,1)} %reduce.5) | data formatting | bytes 294912
  203.9 3.8 %all-to-all-start.1 = ((bf16[16,2,2304]{2,1,0:T(2,128)(2,1)}), bf16[16,2,2304]{2,1,0:T(2,128)(2,1)S(1)}, u32[]{:S(2)}, u32[]{:S(2)}) async-start(bf16[16,2,2304]{2,1,0:T(2,128)(2,1)} %reshape.530), calls=%async_computation.1 | async-start | bytes 294912 | tf_op jit(solution)/shard_map/all_to_all | solution.py:128
  207.7 6.8 %multiply_convert_fusion.1 = (bf16[9,256,96]{1,2,0:T(8,128)(2,1)S(1)}, bf16[9,256,96]{1,2,0:T(8,128)(2,1)S(1)}) fusion(f32[96]{0:T(128)S(1)} %get-tuple-element.51, f32[9,256]{1,0:T(8,128)S(1)} %convert_add_fusion, f32[96]{0:T(128)S(1)} %sqrt.38, f32[96]{0:T(128)S(1)} %get-tuple-element.50), kind=kLoop, calls=%fused_computation.15 | loop fusion | flops 3760128 | bytes 895104 | tf_op jit(solution)/shard_map/convert.3
  214.7 14.5 %reshape.531 = bf16[24576,1,3]{2,1,0:T(2,128)(2,1)} reshape(bf16[16,2,2304]{2,1,0:T(2,128)(2,1)S(1)} %all-to-all-done.1) | data formatting | bytes 294912
  229.2 23.3 %copy.84 = bf16[3,1,24576]{2,0,1:T(4,128)(2,1)S(1)} copy(bf16[3,1,24576]{0,1,2:T(2,128)(2,1)} %bitcast.151) | data formatting | bytes 294912 | tf_op jit(solution)/shard_map/all_to_all | solution.py:128
  254.5 3.1 collective-permute-start.2
  257.7 1.3 collective-permute-start.3
  259.3 3.8 %collective-permute-done.3 = bf16[3,16,1024]{2,1,0:T(8,128)(2,1)S(1)} collective-permute-done((bf16[3,16,1024]{2,1,0:T(8,128)(2,1)S(1)}, bf16[3,16,1024]{2,1,0:T(8,128)(2,1)S(1)}, u32[]{:S(2)}, u32[]{:S(2)}) %collective-permute-start.3) | collective-permute-done | bytes 98336 | tf_op jit(solution)/shard_map/ppermute | solution.py:34
  264.3 75.1 %all_to_all.23 = bf16[3,64,2048]{2,0,1:T(4,128)(2,1)S(1)} all-to-all(bf16[3,64,2048]{2,0,1:T(4,128)(2,1)S(1)} %copy.93), channel_id=1, replica_groups=mesh['space'=32,'tm'=16] {'space'}, dimensions={1} | all-to-all | bytes 1572864 | tf_op jit(solution)/shard_map/all_to_all | solution.py:153
  339.5 1.5 copy.94
  (48 shorter events, 7.7 us)
Async XLA Ops:
  0.0 9.9 %copy-start = (s32[16,2]{0,1:T(2,128)S(1)}, s32[16,2]{0,1:T(2,128)}, u32[]{:S(2)}) copy-start(s32[16,2]{0,1:T(2,128)} %param.10) | copy-start | bytes 388
  1.1 16.9 %collective-permute-start = (bf16[2,3,16,1024]{3,2,1,0:T(8,128)(2,1)S(1)}, bf16[2,3,16,1024]{3,2,1,0:T(8,128)(2,1)S(1)}, u32[]{:S(2)}, u32[]{:S(2)}) collective-permute-start(bf16[2,3,16,1024]{3,2,1,0:T(8,128)(2,1)S(1)} %get-tuple-element.42), channel_id=1, source_target_pairs={{0,1},{1,2},{2,3},{3,4},{4,5},{5,6},{6,7},{7,8},{8,9},{9,10},{10,1... | collective-permute-start | bytes 589832 | tf_op jit(solution)/shard_map/ppermute | solution.py:23
  5.1 12.8 %collective-permute-start.1 = (bf16[2,3,16,1024]{3,2,1,0:T(8,128)(2,1)S(1)}, bf16[2,3,16,1024]{3,2,1,0:T(8,128)(2,1)S(1)}, u32[]{:S(2)}, u32[]{:S(2)}) collective-permute-start(bf16[2,3,16,1024]{3,2,1,0:T(8,128)(2,1)S(1)} %get-tuple-element.43), channel_id=1, source_target_pairs={{1,0},{2,1},{3,2},{4,3},{5,4},{6,5},{7,6},{8,7},{9,8},{10,9},{11,1... | collective-permute-start | bytes 589832 | tf_op jit(solution)/shard_map/ppermute | solution.py:26
  22.6 15.1 %all-to-all-start = ((bf16[2,3,16,1536]{3,0,1,2:T(2,128)(2,1)}), bf16[2,3,16,1536]{3,0,1,2:T(2,128)(2,1)S(1)}, u32[]{:S(2)}, u32[]{:S(2)}) async-start(bf16[2,3,16,1536]{3,0,1,2:T(2,128)(2,1)} %copy.78), calls=%async_computation | async-start | bytes 589824 | tf_op jit(solution)/shard_map/all_to_all | solution.py:123
  193.9 20.6 %copy-start.1 = (s32[16,1]{0,1:T(1,128)S(1)}, s32[16,1]{0,1:T(1,128)}, u32[]{:S(2)}) copy-start(s32[16,1]{0,1:T(1,128)} %param.9) | copy-start | bytes 196
  203.9 10.8 %all-to-all-start.1 = ((bf16[16,2,2304]{2,1,0:T(2,128)(2,1)}), bf16[16,2,2304]{2,1,0:T(2,128)(2,1)S(1)}, u32[]{:S(2)}, u32[]{:S(2)}) async-start(bf16[16,2,2304]{2,1,0:T(2,128)(2,1)} %reshape.530), calls=%async_computation.1 | async-start | bytes 294912 | tf_op jit(solution)/shard_map/all_to_all | solution.py:128
  254.5 4.8 %collective-permute-start.2 = (bf16[3,16,1024]{2,1,0:T(8,128)(2,1)S(1)}, bf16[3,16,1024]{2,1,0:T(8,128)(2,1)S(1)}, u32[]{:S(2)}, u32[]{:S(2)}) collective-permute-start(bf16[3,16,1024]{2,1,0:T(8,128)(2,1)S(1)} %get-tuple-element.41), channel_id=1, source_target_pairs={{0,1},{1,2},{2,3},{3,4},{4,5},{5,6},{6,7},{7,8},{8,9},{9,10},{10,1... | collective-permute-start | bytes 294920 | tf_op jit(solution)/shard_map/ppermute | solution.py:34
  257.7 5.4 %collective-permute-start.3 = (bf16[3,16,1024]{2,1,0:T(8,128)(2,1)S(1)}, bf16[3,16,1024]{2,1,0:T(8,128)(2,1)S(1)}, u32[]{:S(2)}, u32[]{:S(2)}) collective-permute-start(bf16[3,16,1024]{2,1,0:T(8,128)(2,1)S(1)} %get-tuple-element.40), channel_id=1, source_target_pairs={{1,0},{2,1},{3,2},{4,3},{5,4},{6,5},{7,6},{8,7},{9,8},{10,9},{11,1... | collective-permute-start | bytes 294920 | tf_op jit(solution)/shard_map/ppermute | solution.py:34

commit v2 on v1

v2 whole, which is shorter than its diff:
```python
import math

import jax
import jax.numpy as jnp
import ml_dtypes
import numpy as np
from jax import lax
from jax.sharding import PartitionSpec as P

BINS = 96
HOP = 256
HALO = 1024
KERNEL = 2304
TAPS = KERNEL // HOP
WATER = 0.1
EPSILON = 1e-06


def cq_table():
    f32 = np.float32
    octave_bins = BINS // 8
    index = np.arange(BINS).astype(f32)
    freq = f32(0.25) * np.exp2(((index - f32(BINS - 1)) / f32(octave_bins)).astype(np.float64)).astype(f32)
    quality = f32(1.0 / (2.0 ** (1.0 / octave_bins) - 1.0))
    support = np.minimum(quality / freq, f32(KERNEL))
    offset = np.arange(KERNEL).astype(f32) - f32(0.5 * (KERNEL - 1))
    ratio = (offset[:, None] / support[None, :]).astype(np.float64)
    window = np.where(np.abs(ratio) < 0.5, 0.5 + 0.5 * np.cos(2.0 * math.pi * ratio), 0.0)
    window = window / np.sqrt(np.sum(window * window, axis=0, keepdims=True))
    cycles = offset[:, None] * freq[None, :]
    phase = (cycles - np.floor(cycles)).astype(np.float64)
    table = np.concatenate(
        [window * np.cos(2.0 * math.pi * phase), -window * np.sin(2.0 * math.pi * phase)], axis=1
    )
    return table.astype(f32).astype(ml_dtypes.bfloat16)


def shifted(block, distance):
    count = lax.axis_size("tm")
    route = [(i - distance, i) for i in range(count) if 0 <= i - distance < count]
    return lax.ppermute(block, "tm", route)


def on_device(recordings, owner, valid_range, bin_mask):
    table = jnp.asarray(cq_table())
    margin = HALO // HOP
    comps, rec_dev, samples_dev = recordings.shape[1:]
    frames = samples_dev // HOP
    rows = comps * rec_dev
    blocks = recordings.reshape(2, rows, frames, HOP).transpose(0, 2, 1, 3)
    low = shifted(blocks[:, frames - margin :], 1)
    high = shifted(blocks[:, :margin], -1)
    ext = jnp.concatenate([low, blocks, high], axis=1)
    unfolded = jnp.concatenate([ext[:, tap : tap + frames] for tap in range(TAPS)], axis=-1)
    coefs = jnp.einsum("sfrh,hk->sfrk", unfolded, table, preferred_element_type=jnp.float32)
    coefs = coefs.astype(jnp.bfloat16).astype(jnp.float32)
    obs = coefs[1]
    frames_all = frames * lax.axis_size("tm")
    power = lax.psum(jnp.sum(obs * obs, axis=(0, 2)), "tm")
    level = (WATER * (power / (frames_all * BINS)) + EPSILON)[None, :, None]
    first = lax.axis_index("tm") * frames
    centers = (first + jnp.arange(frames, dtype=jnp.int32)) * HOP + HOP // 2
    inside = (valid_range[None, :, 0] <= centers[:, None]) & (centers[:, None] < valid_range[None, :, 1])
    weight = inside.astype(jnp.float32)[:, :, None] * bin_mask.astype(jnp.float32)[None]
    weight = jnp.tile(weight, (1, comps, 1))
    x_re, x_im = coefs[0, ..., :BINS], coefs[0, ..., BINS:]
    y_re, y_im = obs[..., :BINS], obs[..., BINS:]
    x_norm = jnp.sqrt(x_re * x_re + x_im * x_im + level)
    y_norm = jnp.sqrt(y_re * y_re + y_im * y_im + level)
    d_re = weight * (x_re / x_norm - y_re / y_norm)
    d_im = weight * (x_im / x_norm - y_im / y_norm)
    inner = (x_re * d_re + x_im * d_im) / (x_norm * x_norm * x_norm)
    adjoint = jnp.concatenate([d_re / x_norm - x_re * inner, d_im / x_norm - x_im * inner], axis=-1)
    adjoint = adjoint.astype(jnp.bfloat16)
    term = jnp.einsum("frk,hk->frh", adjoint, table, preferred_element_type=jnp.float32)
    flat = sum(
        jnp.pad(term[..., tap * HOP : (tap + 1) * HOP], ((tap, TAPS - 1 - tap), (0, 0), (0, 0)))
        for tap in range(TAPS)
    )
    middle = flat[margin : margin + frames]
    before = shifted(flat[margin + frames :].astype(jnp.bfloat16), 1).astype(jnp.float32)
    after = shifted(flat[:margin].astype(jnp.bfloat16), -1).astype(jnp.float32)
    middle = middle + jnp.concatenate([before, after], axis=0)
    series = middle.astype(jnp.bfloat16).reshape(frames, comps, rec_dev, HOP)
    count = lax.axis_size("space")
    most = max(2, 3 * rec_dev // (2 * count))
    target = owner[:, 0]
    place = jnp.arange(rec_dev, dtype=jnp.int32)
    earlier = (target[:, None] == target[None, :]) & (place[None, :] < place[:, None])
    slot = target * most + jnp.sum(earlier.astype(jnp.int32), axis=1)
    select = (jnp.arange(count * most, dtype=jnp.int32)[:, None] == slot[None, :]).astype(jnp.bfloat16)
    outgoing = jnp.einsum("sr,fcrh->cfsh", select, series, preferred_element_type=jnp.float32)
    outgoing = outgoing.astype(jnp.bfloat16).transpose(0, 2, 1, 3).reshape(comps, count * most, samples_dev)
    return lax.all_to_all(outgoing, "space", split_axis=1, concat_axis=1, tiled=True)


def solution(mesh):
    return jax.shard_map(
        on_device,
        mesh=mesh,
        in_specs=(
            P(None, None, "space", "tm"),
            P("space", None),
            P("space", None),
            P("space", None),
        ),
        out_specs=P(None, "space", "tm"),
        check_vma=False,
    )
```

time: 343 us -> 138 us (0.40)
  other arithmetic: 157 us -> 3.07 us
  local copies, waits for them, and re-layouts: 75.3 us -> 4.83 us
  blocking collectives: 75.1 us -> 113 us
  starting transfers between devices: 21.1 us -> 7.92 us
  waiting for transfers between devices: 10.2 us -> 6.36 us
    unnamed x1 -> x7, other arithmetic: 135 us -> 0.19 us
    psum x0 -> x1, blocking collectives: none -> 32.7 us  [on_device(): power = lax.psum(jnp.sum(obs * obs, axis=(0, 2)), 'tm')]
    unnamed x16 -> x8, local copies, waits for them, and re-layouts: 26 us -> 1.17 us
    all_to_all x1 -> x0, local copies, waits for them, and re-layouts: 23.3 us -> none  [on_device(): lax.all_to_all(adjoint_local, 'tm', split_axis=2, concat_axis=1, tiled=True)]
    convert_element_type x4 -> x0, local copies, waits for them, and re-layouts: 20.6 us -> none  [the longest x2 19.7 us: misfit(): joined.reshape(joined.shape[:2] + (joined.shape[2] * joined.shape[3],))]
    another operation x4 -> x3, other arithmetic: 13.9 us -> 0.87 us
    all_to_all x2 -> x0, starting transfers between devices: 11.3 us -> none  [the longest x1 7.54 us: on_device(): lax.all_to_all(packed, 'tm', split_axis=2, concat_axis=3, tiled=True)]
    all_to_all x2 -> x0, waiting for transfers between devices: 6.19 us -> none  [the longest x1 6.19 us: on_device(): lax.all_to_all(packed, 'tm', split_axis=2, concat_axis=3, tiled=True)]
  transfers between devices with their start and end apart: 6 -> 4, of which waited for: 3 -> 3; matrix products, arithmetic and copies ran while one was open for 6% -> 2% of each run, Pallas kernels for 0% -> 0%
where the time goes in v2:
time: 138 us
  blocking collectives  113 us (82%)
  starting transfers between devices  7.92 us (6%)
  waiting for transfers between devices  6.36 us (5%)
  local copies, waits for them, and re-layouts  4.83 us (4%)
  other arithmetic  3.07 us (2%)
  matrix products  2.25 us (2%)
    all_to_all x1, blocking collectives, on_device(): lax.all_to_all(outgoing, 'space', split_axis=1, concat_axis=1, tiled=True)  80.6 us
    psum x1, blocking collectives, on_device(): power = lax.psum(jnp.sum(obs * obs, axis=(0, 2)), 'tm')  32.7 us
    ppermute x4, starting transfers between devices, shifted(): return lax.ppermute(block, 'tm', route)  7.92 us
    ppermute x4, waiting for transfers between devices, shifted(): return lax.ppermute(block, 'tm', route)  6.36 us
  transfers between devices with their start and end apart: 4, of which 3 were waited for; matrix products, arithmetic and copies ran while one was open for 2% of the time, Pallas kernels for 0%

profile of v2, /device:TPU:1, one launch (start us, length us, event | category | flops | bytes accessed | tf_op | source)
XLA Modules:
  0.0 138.1 jit_solution(9052175002597271210)
XLA Ops:
  0.0 1.1 copy.20
  1.2 4.0 %collective-permute-start = (bf16[2,4,48,256]{3,2,1,0:T(8,128)(2,1)S(1)}, bf16[2,4,48,256]{3,2,1,0:T(8,128)(2,1)S(1)}, u32[]{:S(2)}, u32[]{:S(2)}) collective-permute-start(bf16[2,4,48,256]{3,2,1,0:T(8,128)(2,1)S(1)} %get-tuple-element.22), channel_id=1, source_target_pairs={{0,1},{1,2},{2,3},{3,4},{4,5},{5,6},{6,7},{7,8},{8,9},{9,10},{10,1... | collective-permute-start | bytes 589832 | tf_op jit(solution)/shard_map/ppermute | solution.py:41
  5.2 1.3 collective-permute-start.1
  6.5 0.8 slice_bitcast_fusion.4
  7.3 0.7 convert_element_type.54
  8.0 0.9 convert_reduce_fusion
  9.3 2.3 %collective-permute-done.1 = bf16[2,4,48,256]{3,2,1,0:T(8,128)(2,1)S(1)} collective-permute-done((bf16[2,4,48,256]{3,2,1,0:T(8,128)(2,1)S(1)}, bf16[2,4,48,256]{3,2,1,0:T(8,128)(2,1)S(1)}, u32[]{:S(2)}, u32[]{:S(2)}) %collective-permute-start.1) | collective-permute-done | bytes 196640 | tf_op jit(solution)/shard_map/ppermute | solution.py:41
  11.8 1.1 fusion.1
  13.0 0.1 multiply_reduce_fusion
  13.1 32.7 %psum.7 = f32[48]{0:T(128)S(1)} all-reduce(f32[48]{0:T(128)S(1)} %multiply_reduce_fusion), channel_id=1, replica_groups=mesh['space'=32,'tm'=16] {'tm'}, use_global_device_ids=true, to_apply=%region_1.0 | all-reduce | flops 48 | bytes 384 | tf_op jit(solution)/shard_map/psum | solution.py:59
  45.8 0.4 subtract_convert_fusion.1
  46.2 0.2 subtract_convert_fusion
  46.5 0.7 fusion.18
  47.1 0.5 fusion.28
  47.6 0.3 fusion.27
  47.9 1.3 collective-permute-start.2
  49.3 1.3 collective-permute-start.3
  50.6 0.3 collective-permute-done.2
  50.9 3.7 %collective-permute-done.3 = bf16[4,48,256]{2,1,0:T(8,128)(2,1)S(1)} collective-permute-done((bf16[4,48,256]{2,1,0:T(8,128)(2,1)S(1)}, bf16[4,48,256]{2,1,0:T(8,128)(2,1)S(1)}, u32[]{:S(2)}, u32[]{:S(2)}) %collective-permute-start.3) | collective-permute-done | bytes 98336 | tf_op jit(solution)/shard_map/ppermute | solution.py:41
  54.7 0.5 fusion
  55.2 0.4 copy.18
  55.6 0.4 reshape.94
  56.0 80.6 %all_to_all.5 = bf16[3,64,2048]{2,0,1:T(4,128)(2,1)S(1)} all-to-all(bf16[3,64,2048]{2,0,1:T(4,128)(2,1)S(1)} %reshape.94), channel_id=1, replica_groups=mesh['space'=32,'tm'=16] {'space'}, dimensions={1} | all-to-all | bytes 1572864 | tf_op jit(solution)/shard_map/all_to_all | solution.py:94
  136.6 1.5 %copy.15 = bf16[3,64,2048]{2,1,0:T(8,128)(2,1)} copy(bf16[3,64,2048]{2,0,1:T(4,128)(2,1)S(1)} %all_to_all.5) | data formatting | bytes 1572864 | tf_op jit(solution)/shard_map/all_to_all | solution.py:94
  (26 shorter events, 0.7 us)
Async XLA Ops:
  1.2 7.9 %collective-permute-start = (bf16[2,4,48,256]{3,2,1,0:T(8,128)(2,1)S(1)}, bf16[2,4,48,256]{3,2,1,0:T(8,128)(2,1)S(1)}, u32[]{:S(2)}, u32[]{:S(2)}) collective-permute-start(bf16[2,4,48,256]{3,2,1,0:T(8,128)(2,1)S(1)} %get-tuple-element.22), channel_id=1, source_target_pairs={{0,1},{1,2},{2,3},{3,4},{4,5},{5,6},{6,7},{7,8},{8,9},{9,10},{10,1... | collective-permute-start | bytes 589832 | tf_op jit(solution)/shard_map/ppermute | solution.py:41
  5.2 6.4 %collective-permute-start.1 = (bf16[2,4,48,256]{3,2,1,0:T(8,128)(2,1)S(1)}, bf16[2,4,48,256]{3,2,1,0:T(8,128)(2,1)S(1)}, u32[]{:S(2)}, u32[]{:S(2)}) collective-permute-start(bf16[2,4,48,256]{3,2,1,0:T(8,128)(2,1)S(1)} %get-tuple-element.21), channel_id=1, source_target_pairs={{1,0},{2,1},{3,2},{4,3},{5,4},{6,5},{7,6},{8,7},{9,8},{10,9},{11,1... | collective-permute-start | bytes 589832 | tf_op jit(solution)/shard_map/ppermute | solution.py:41
  9.2 2.6 %copy-start.2 = (bf16[2304,192,1,1]{0,1,3,2:T(8,128)(2,1)S(1)}, bf16[2304,192,1,1]{0,1,3,2:T(8,128)(2,1)}, u32[]{:S(2)}) copy-start(bf16[2304,192,1,1]{0,1,3,2:T(8,128)(2,1)} %constant.49) | copy-start | bytes 2654212
  11.8 34.6 %copy-start = (bf16[2304,192,1]{0,1,2:T(8,128)(2,1)S(1)}, bf16[2304,192,1]{0,1,2:T(8,128)(2,1)}, u32[]{:S(2)}) copy-start(bf16[2304,192,1]{0,1,2:T(8,128)(2,1)} %constant.50) | copy-start | bytes 2654212
  47.6 2.9 %copy-start.1 = (s32[16,1]{0,1:T(1,128)S(1)}, s32[16,1]{0,1:T(1,128)}, u32[]{:S(2)}) copy-start(s32[16,1]{0,1:T(1,128)} %param.6) | copy-start | bytes 196
  47.9 2.9 %collective-permute-start.2 = (bf16[4,48,256]{2,1,0:T(8,128)(2,1)S(1)}, bf16[4,48,256]{2,1,0:T(8,128)(2,1)S(1)}, u32[]{:S(2)}, u32[]{:S(2)}) collective-permute-start(bf16[4,48,256]{2,1,0:T(8,128)(2,1)S(1)} %get-tuple-element.19), channel_id=1, source_target_pairs={{0,1},{1,2},{2,3},{3,4},{4,5},{5,6},{6,7},{7,8},{8,9},{9,10},{10,1... | collective-permute-start | bytes 294920 | tf_op jit(solution)/shard_map/ppermute | solution.py:41
  49.3 5.4 %collective-permute-start.3 = (bf16[4,48,256]{2,1,0:T(8,128)(2,1)S(1)}, bf16[4,48,256]{2,1,0:T(8,128)(2,1)S(1)}, u32[]{:S(2)}, u32[]{:S(2)}) collective-permute-start(bf16[4,48,256]{2,1,0:T(8,128)(2,1)S(1)} %get-tuple-element.20), channel_id=1, source_target_pairs={{1,0},{2,1},{3,2},{4,3},{5,4},{6,5},{7,6},{8,7},{9,8},{10,9},{11,1... | collective-permute-start | bytes 294920 | tf_op jit(solution)/shard_map/ppermute | solution.py:41

commit v3 on v2

v3 whole, which is shorter than its diff:
```python
import functools
import math

import jax
import jax.numpy as jnp
import ml_dtypes
import numpy as np
from jax import lax
from jax.experimental import pallas as pl
from jax.experimental.pallas import tpu as pltpu
from jax.sharding import PartitionSpec as P

BINS = 96
HOP = 256
HALO = 1024
KERNEL = 2304
TAPS = KERNEL // HOP
MARGIN = HALO // HOP
WATER = 0.1
EPSILON = 1e-06
MOST = 2
LANES = 128
MESH = pl.DeviceIdType.MESH


def cq_table():
    f32 = np.float32
    octave_bins = BINS // 8
    index = np.arange(BINS).astype(f32)
    freq = f32(0.25) * np.exp2(((index - f32(BINS - 1)) / f32(octave_bins)).astype(np.float64)).astype(f32)
    quality = f32(1.0 / (2.0 ** (1.0 / octave_bins) - 1.0))
    support = np.minimum(quality / freq, f32(KERNEL))
    offset = np.arange(KERNEL).astype(f32) - f32(0.5 * (KERNEL - 1))
    ratio = (offset[:, None] / support[None, :]).astype(np.float64)
    window = np.where(np.abs(ratio) < 0.5, 0.5 + 0.5 * np.cos(2.0 * math.pi * ratio), 0.0)
    window = window / np.sqrt(np.sum(window * window, axis=0, keepdims=True))
    cycles = offset[:, None] * freq[None, :]
    phase = (cycles - np.floor(cycles)).astype(np.float64)
    table = np.zeros((KERNEL, 2 * LANES))
    table[:, :BINS] = window * np.cos(2.0 * math.pi * phase)
    table[:, LANES : LANES + BINS] = -window * np.sin(2.0 * math.pi * phase)
    return table.astype(f32).astype(ml_dtypes.bfloat16)


def ring_rows(chips, rec_dev):
    half = chips // 2
    return [min(rec_dev, 2 * MOST * (half - k) + MOST) for k in range(1, half + 1)]


def kernel(
    sizes, rec_in, owner, valid, mask, table_in, out, rec, table, bins, across,
    ext, coef, adj, acc, lv_out, lv_in, meta_out, meta_in, order, meta_s, order_s,
    edge_out, edge_in, flat, rows, packet, mate_out, mate_in, slots,
    halo_send, halo_recv, one_send, one_recv, edge_send, edge_recv, ring_send, ring_recv, mate_recv, local, *bufs,
):
    chips, groups, comps, rec_dev, frames = sizes
    half = chips // 2
    traces = comps * rec_dev
    per_row = frames * HOP // LANES
    hops = ring_rows(chips, rec_dev)
    f32, i32 = jnp.float32, jnp.int32

    space, t = lax.axis_index("space"), lax.axis_index("tm")
    z, core = space // 2, space % 2

    def band(d):
        return {"tm": lax.rem(t + d + groups, groups)}

    def chip(d):
        return {"space": lax.rem(z + d + chips, chips) * 2 + core}

    mate = {"space": z * 2 + 1 - core}

    def send(src, dst, ss, rs, to):
        copy = pltpu.make_async_remote_copy(src, dst, ss, rs, device_id=to, device_id_type=MESH)
        copy.start()
        return copy

    def wait_bytes(ref, sem):
        pltpu.make_async_copy(ref, ref, sem).wait()

    barrier = pltpu.get_barrier_semaphore()
    others = [band(d) for d in range(1, groups)] + [chip(d) for d in range(1, chips)] + [mate]
    for to in others:
        pl.semaphore_signal(barrier, inc=1, device_id=to, device_id_type=MESH)

    rec_copy = pltpu.make_async_copy(rec_in, rec, local.at[3])
    rec_copy.start()
    table_copy = pltpu.make_async_copy(table_in, table, local.at[4])
    table_copy.start()

    lane = lax.broadcasted_iota(i32, (rec_dev, LANES), 1)
    line = lax.broadcasted_iota(i32, (rec_dev, LANES), 0)
    listed = lane < rec_dev

    def widened(ref, n):
        across[n : n + 1, pl.ds(0, rec_dev)] = ref[n : n + 1, :]
        return jnp.broadcast_to(across[n : n + 1, :], (rec_dev, LANES))

    def upright(values):
        return jnp.broadcast_to(jnp.sum(jnp.where(line == lane, values, 0), axis=1, keepdims=True), (rec_dev, LANES))

    across[...] = jnp.zeros_like(across)
    own_t = widened(owner, 0)
    own = upright(own_t)
    first, last = upright(widened(valid, 0)), upright(widened(valid, 1))
    bins[...] = jnp.zeros_like(bins)
    bins[:, pl.ds(0, BINS)] = mask[...].astype(f32)
    before = listed & (lane < line)

    def count(what):
        return jnp.broadcast_to(jnp.sum(jnp.where(what, 1, 0), axis=1, keepdims=True), (rec_dev, LANES))

    def count_t(what):
        return jnp.broadcast_to(jnp.sum(jnp.where(what, 1, 0), axis=0, keepdims=True), (rec_dev, LANES))

    far = lax.rem(own // 2 + chips - z, chips)
    far_t = lax.rem(own_t // 2 + chips - z, chips)
    rank = count(before & (own_t == own))
    turn = count(before & (far_t == half))
    turn_t = count_t((line < lane) & (far == half))
    up = ((far > 0) & (far < half)) | ((far == half) & (turn % 2 == 0))
    up_t = ((far_t > 0) & (far_t < half)) | ((far_t == half) & (turn_t % 2 == 0))
    down = (far > half) | ((far == half) & (turn % 2 == 1))
    down_t = (far_t > half) | ((far_t == half) & (turn_t % 2 == 1))
    same = before & (far_t == far)
    place_up = count(listed & up_t & ((far_t > far) | same))
    place_down = count(listed & down_t & ((far_t < far) | same))
    place = jnp.where(up, place_up, jnp.where(down, rec_dev + place_down, line))
    key = far * (2 * MOST) + (own % 2) * MOST + rank
    sent = jnp.sum(jnp.where(key == lane, place + 1, 0), axis=0, keepdims=True)
    meta_out[...] = jnp.broadcast_to(sent, meta_out.shape)
    taken = jnp.sum(jnp.where((place == lane) & (up | down), line, 0), axis=0, keepdims=True)
    order[...] = jnp.broadcast_to(taken, order.shape)
    order_copy = pltpu.make_async_copy(order, order_s, local.at[0])
    order_copy.start()
    own_copy = pltpu.make_async_copy(meta_out, meta_s.at[0], local.at[1])
    own_copy.start()

    rec_copy.wait()
    for s in (1, 0):
        for b in range(frames):
            for c in range(comps):
                ext[s, MARGIN + b, pl.ds(c * rec_dev, rec_dev), :] = rec[s, c, :, pl.ds(b * HOP, HOP)]

    pl.semaphore_wait(barrier, len(others))

    halo = []
    for i, s in enumerate((1, 0)):
        halo.append(send(ext.at[s, pl.ds(frames, MARGIN)], ext.at[s, pl.ds(0, MARGIN)],
                         halo_send.at[2 * i], halo_recv.at[2 * i], band(1)))
        halo.append(send(ext.at[s, pl.ds(MARGIN, MARGIN)], ext.at[s, pl.ds(MARGIN + frames, MARGIN)],
                         halo_send.at[2 * i + 1], halo_recv.at[2 * i + 1], band(-1)))
    for d in range(1, chips):
        send(meta_out, meta_in.at[d - 1], one_send.at[0], one_recv.at[0], chip(d))

    def analyse(s):
        total = None
        for tap in range(TAPS):
            term = jnp.dot(
                ext[s, pl.ds(tap, frames)].reshape(frames * traces, HOP),
                table[pl.ds(tap * HOP, HOP), :],
                preferred_element_type=f32,
            )
            total = term if total is None else total + term
        coef[s] = total.astype(jnp.bfloat16)

    def take_halo(i, s):
        halo[2 * i].wait_recv()
        halo[2 * i + 1].wait_recv()

        @pl.when(t == 0)
        def _():
            ext[s, pl.ds(0, MARGIN)] = jnp.zeros((MARGIN, traces, HOP), jnp.bfloat16)

        @pl.when(t == groups - 1)
        def _():
            ext[s, pl.ds(MARGIN + frames, MARGIN)] = jnp.zeros((MARGIN, traces, HOP), jnp.bfloat16)

    table_copy.wait()
    take_halo(0, 1)
    analyse(1)
    diagonal = lax.broadcasted_iota(i32, (traces, LANES), 0) == lax.broadcasted_iota(i32, (traces, LANES), 1)
    power = jnp.zeros((traces, LANES), f32)
    for f in range(frames):
        o = coef[1, pl.ds(f * traces, traces), :].astype(f32)
        power = power + (o[:, :LANES] * o[:, :LANES] + o[:, LANES:] * o[:, LANES:])
    power = jnp.broadcast_to(jnp.sum(power, axis=1, keepdims=True), (traces, LANES))
    power = jnp.sum(jnp.where(diagonal, power, 0.0), axis=0, keepdims=True)
    lv_out[...] = jnp.broadcast_to(power, lv_out.shape)
    for d in range(1, groups):
        send(lv_out, lv_in.at[d - 1], one_send.at[1], one_recv.at[1], band(d))

    take_halo(1, 0)
    analyse(0)

    wait_bytes(lv_in, one_recv.at[1])
    power = lv_out[...]
    for d in range(1, groups):
        power = power + lv_in[d - 1]
    power = jnp.broadcast_to(power[0:1], (traces, LANES))
    power = jnp.sum(jnp.where(diagonal, power, 0.0), axis=1, keepdims=True)
    level = jnp.broadcast_to(WATER * (power / (frames * groups * BINS)) + EPSILON, (traces, LANES))

    first, last, bands = (jnp.concatenate([v] * comps, axis=0) for v in (first, last, bins[...]))
    for f in range(frames):
        center = (t * frames + f) * HOP + HOP // 2
        weight = jnp.where((first <= center) & (center < last), bands, 0.0)
        x = coef[0, pl.ds(f * traces, traces), :].astype(f32)
        y = coef[1, pl.ds(f * traces, traces), :].astype(f32)
        x_re, x_im, y_re, y_im = x[:, :LANES], x[:, LANES:], y[:, :LANES], y[:, LANES:]
        x_inv = lax.rsqrt(x_re * x_re + x_im * x_im + level)
        y_inv = lax.rsqrt(y_re * y_re + y_im * y_im + level)
        d_re = weight * (x_re * x_inv - y_re * y_inv)
        d_im = weight * (x_im * x_inv - y_im * y_inv)
        inner = (x_re * d_re + x_im * d_im) * (x_inv * x_inv * x_inv)
        adj[pl.ds(f * traces, traces), pl.ds(0, LANES)] = (d_re * x_inv - x_re * inner).astype(jnp.bfloat16)
        adj[pl.ds(f * traces, traces), pl.ds(LANES, LANES)] = (d_im * x_inv - x_im * inner).astype(jnp.bfloat16)

    acc[...] = jnp.zeros_like(acc)
    for tap in range(TAPS):
        term = lax.dot_general(
            adj[...], table[pl.ds(tap * HOP, HOP), :], (((1,), (1,)), ((), ())), preferred_element_type=f32
        )
        acc[pl.ds(tap, frames)] += term.reshape(frames, traces, HOP)
    edge_out[0] = acc[pl.ds(MARGIN + frames, MARGIN)].astype(jnp.bfloat16)
    edge_out[1] = acc[pl.ds(0, MARGIN)].astype(jnp.bfloat16)
    edges = [
        send(edge_out.at[i], edge_in.at[i], edge_send.at[i], edge_recv.at[i], band(1 - 2 * i)) for i in range(2)
    ]
    for edge in edges:
        edge.wait_recv()
    for b in range(frames):
        side, i = (0, b) if b < MARGIN else (1, b - MARGIN)
        inner_band = (t > 0) if side == 0 else (t < groups - 1)
        more = jnp.where(inner_band, edge_in[side, i].astype(f32), 0.0)
        block = acc[MARGIN + b] + more
        for h in range(HOP // LANES):
            j = b * (HOP // LANES) + h
            flat[pl.ds(j * traces, traces), :] = block[:, h * LANES : (h + 1) * LANES]

    order_copy.wait()
    own_copy.wait()
    for c in range(comps):
        for r in range(rec_dev):
            row = flat[pl.ds(c * rec_dev + r, per_row, stride=traces), :]
            rows[c, r] = row.astype(jnp.bfloat16)
    flying = {}

    def hop(k, c, i):
        src = packet.at[i, c] if k == 1 else bufs[2 * (k - 2) + i].at[c, pl.ds(0, hops[k - 1])]
        n = ((k - 1) * comps + c) * 2 + i
        flying[k, c, i] = send(src, bufs[2 * (k - 1) + i].at[c], ring_send.at[n], ring_recv.at[n], chip(1 - 2 * i))

    for c in range(comps):
        for i in range(2):
            for p in range(rec_dev):
                packet[i, c, p] = rows[c, order_s[0, i * rec_dev + p]]
            hop(1, c, i)

    wait_bytes(meta_in, one_recv.at[0])
    got = pltpu.make_async_copy(meta_in, meta_s.at[pl.ds(1, chips - 1)], local.at[2])
    got.start()
    got.wait()

    def keep(source, rank, c, row):
        slot = (lax.rem(z + source + chips, chips) * 2 + core) * MOST + rank
        slots[pl.ds(pl.multiple_of((slot * comps + c) * per_row, per_row), per_row), :] = row.astype(f32)

    def deal(source, j, read):
        for e in range(2 * MOST):
            mine, rank = e // MOST == 0, e % MOST
            whose = core if mine else 1 - core
            away = (-source) % chips
            v = meta_s[away, 0, away * 2 * MOST + whose * MOST + rank]
            for c in range(comps):
                row = jnp.where(v > 0, read(c, v), jnp.zeros((), jnp.bfloat16))
                if mine:
                    keep(source, rank, c, row)
                else:
                    mate_out[j, rank, c] = row

    def from_ring(k, i):
        def read(c, v):
            at = jnp.clip(v - 1 - i * rec_dev, 0, hops[k - 1] - 1)
            return bufs[2 * (k - 1) + i][c, at]

        return read

    def from_both(c, v):
        return jnp.where(v > rec_dev, from_ring(half, 1)(c, v), from_ring(half, 0)(c, v))

    deal(0, 0, lambda c, v: rows[c, jnp.clip(v - 1, 0, rec_dev - 1)])
    mates = []

    def to_mate(first_j, number):
        ref = (mate_out.at[pl.ds(first_j, number)], mate_in.at[pl.ds(first_j, number)])
        mates.append((first_j, number, send(*ref, one_send.at[2], mate_recv.at[len(mates)], mate)))

    for k in range(2, half + 2):
        for c in range(comps):
            for i in range(2):
                flying[k - 1, c, i].wait_recv()
                if k <= half:
                    hop(k, c, i)
        if k <= half:
            for i in range(2):
                deal(1 - k if i == 0 else k - 1, 2 * (k - 1) - 1 + i, from_ring(k - 1, i))
            if k % 2 == 0:
                to_mate(2 * (k - 2) - 1 if k > 2 else 0, 4 if k > 2 else 3)
        else:
            deal(half, 2 * half - 1, from_both)
            to_mate(2 * half - 1, 1)
    source_of = [0] + [s for k in range(1, half) for s in (-k, k)] + [half]
    for first_j, number, copy in mates:
        copy.wait_recv()
        for j in range(first_j, first_j + number):
            for rank in range(MOST):
                slot = (lax.rem(z + source_of[j] + chips, chips) * 2 + 1 - core) * MOST + rank
                for c in range(comps):
                    slots[pl.ds(pl.multiple_of((slot * comps + c) * per_row, per_row), per_row), :] = (
                        mate_in[j, rank, c].astype(f32)
                    )
    kept = chips * 2 * MOST
    for c in range(comps):
        for j in range(per_row):
            part = slots[pl.ds(c * per_row + j, kept, stride=comps * per_row), :]
            out[c, :, pl.ds(j * LANES, LANES)] = part.astype(jnp.bfloat16)

    for copy in halo + edges + list(flying.values()):
        copy.wait_send()
    wait_bytes(meta_in, one_send.at[0])
    wait_bytes(lv_in, one_send.at[1])
    wait_bytes(mate_out, one_send.at[2])


def solution(mesh):
    chips, groups = mesh.shape["space"] // 2, mesh.shape["tm"]

    def on_device(recordings, owner, valid_range, bin_mask):
        _, comps, rec_dev, samples = recordings.shape
        frames = samples // HOP
        traces, per_row = comps * rec_dev, samples // LANES
        kept = chips * 2 * MOST
        bf16, f32, i32 = jnp.bfloat16, jnp.float32, jnp.int32
        sizes = (chips, groups, comps, rec_dev, frames)
        dma = pltpu.SemaphoreType.DMA
        return pl.pallas_call(
            functools.partial(kernel, sizes),
            out_shape=jax.ShapeDtypeStruct((comps, kept, samples), bf16),
            in_specs=[pl.BlockSpec(memory_space=space) for space in (pl.ANY, pltpu.VMEM, pltpu.VMEM, pltpu.VMEM, pl.ANY)],
            out_specs=pl.BlockSpec(memory_space=pltpu.VMEM),
            scratch_shapes=[
                pltpu.VMEM(recordings.shape, bf16),
                pltpu.VMEM((KERNEL, 2 * LANES), bf16),
                pltpu.VMEM((rec_dev, LANES), f32),
                pltpu.VMEM((8, LANES), i32),
                pltpu.VMEM((2, frames + 2 * MARGIN, traces, HOP), bf16),
                pltpu.VMEM((2, frames * traces, 2 * LANES), bf16),
                pltpu.VMEM((frames * traces, 2 * LANES), bf16),
                pltpu.VMEM((frames + 2 * MARGIN, traces, HOP), f32),
                pltpu.VMEM((8, LANES), f32),
                pltpu.VMEM((groups - 1, 8, LANES), f32),
                pltpu.VMEM((8, LANES), i32),
                pltpu.VMEM((chips - 1, 8, LANES), i32),
                pltpu.VMEM((8, LANES), i32),
                pltpu.SMEM((chips, 8, LANES), i32),
                pltpu.SMEM((8, LANES), i32),
                pltpu.VMEM((2, MARGIN, traces, HOP), bf16),
                pltpu.VMEM((2, MARGIN, traces, HOP), bf16),
                pltpu.VMEM((per_row * traces, LANES), f32),
                pltpu.VMEM((comps, rec_dev, per_row, LANES), bf16),
                pltpu.VMEM((2, comps, rec_dev, per_row, LANES), bf16),
                pltpu.VMEM((chips, MOST, comps, per_row, LANES), bf16),
                pltpu.VMEM((chips, MOST, comps, per_row, LANES), bf16),
                pltpu.VMEM((kept * comps * per_row, LANES), f32),
                dma((4,)), dma((4,)), dma((3,)), dma((2,)), dma((2,)), dma((2,)),
                dma((chips * comps,)), dma((chips * comps,)), dma((chips // 4 + 1,)), dma((5,)),
            ] + [pltpu.VMEM((comps, n, per_row, LANES), bf16) for n in ring_rows(chips, rec_dev) for _ in range(2)],
            compiler_params=pltpu.CompilerParams(
                collective_id=0, has_side_effects=True, vmem_limit_bytes=60 << 20
            ),
        )(recordings, owner.T, valid_range.T, bin_mask, jnp.asarray(cq_table()))

    return jax.shard_map(
        on_device,
        mesh=mesh,
        in_specs=(
            P(None, None, "space", "tm"),
            P("space", None),
            P("space", None),
            P("space", None),
        ),
        out_specs=P(None, "space", "tm"),
        check_vma=False,
    )
```

time: 138 us -> 75.3 us (0.55)
  blocking collectives: 113 us -> 0 us
  Pallas kernels: 0 us -> 73 us
  starting transfers between devices: 7.92 us -> 0 us
  waiting for transfers between devices: 6.36 us -> 0 us
  other arithmetic: 3.07 us -> 0 us
  local copies, waits for them, and re-layouts: 4.83 us -> 2.09 us
  matrix products: 2.25 us -> 0 us
    all_to_all x1 -> x0, blocking collectives: 80.6 us -> none  [on_device(): lax.all_to_all(outgoing, 'space', split_axis=1, concat_axis=1, tiled=True)]
    pallas_call x0 -> x1, Pallas kernels: none -> 73 us  [on_device(): pl.pallas_call(functools.partial(kernel, sizes), out_shape=jax.ShapeDtype...]
    psum x1 -> x0, blocking collectives: 32.7 us -> none  [on_device(): power = lax.psum(jnp.sum(obs * obs, axis=(0, 2)), 'tm')]
    ppermute x4 -> x0, starting transfers between devices: 7.92 us -> none  [shifted(): return lax.ppermute(block, 'tm', route)]
    ppermute x4 -> x0, waiting for transfers between devices: 6.36 us -> none  [shifted(): return lax.ppermute(block, 'tm', route)]
    dot_general x3 -> x0, matrix products: 2.25 us -> none  [the longest x1 1.09 us: on_device(): jnp.einsum('sfrh,hk->sfrk', unfolded, table, preferred_element_type=jnp.f...]
    all_to_all x1 -> x0, local copies, waits for them, and re-layouts: 1.45 us -> none  [on_device(): lax.all_to_all(outgoing, 'space', split_axis=1, concat_axis=1, tiled=True)]
  transfers between devices with their start and end apart: 4 -> 0, of which waited for: 3 -> 0; matrix products, arithmetic and copies ran while one was open for 2% -> 0% of each run, Pallas kernels for 0% -> 0%
where the time goes in v3:
time: 75.3 us; the launch traced here: 75.1 us
  Pallas kernels  73 us (97%)
  local copies, waits for them, and re-layouts  2.09 us (3%)
    pallas_call x1, Pallas kernels, on_device(): pl.pallas_call(functools.partial(kernel, sizes), out_shape=jax.ShapeDtype...  73 us
    unnamed x1, local copies, waits for them, and re-layouts  2.09 us

profile of v3, /device:TPU:1, one launch (start us, length us, event | category | flops | bytes accessed | tf_op | source)
XLA Modules:
  0.0 75.1 jit_solution(11749757222319888356)
XLA Ops:
  0.0 73.0 %shard_map.55 = bf16[3,64,2048]{2,1,0:T(8,128)(2,1)} custom-call(bf16[2,3,16,2048]{3,2,1,0:T(8,128)(2,1)} %rec_in.1, s32[1,16]{1,0:T(1,128)} %bitcast.3, s32[2,16]{1,0:T(2,128)} %bitcast.2, s32[16,96]{1,0:T(8,128)} %mask.1, bf16[2304,256]{1,0:T(8,128)(2,1)} %constant.2.clone.table_in), custom_call_target="tpu_custom_call" | custom-call | tf_op jit(solution)/shard_map/pallas_call | solution.py:348
  73.0 2.1 %copy.7 = bf16[3,64,2048]{2,1,0:T(8,128)(2,1)} copy(bf16[3,64,2048]{2,1,0:T(8,128)(2,1)} %shard_map.55) | data formatting | bytes 1572864

commit v4 on v3

v4 whole, which is shorter than its diff:
```python
import functools
import math

import jax
import jax.numpy as jnp
import ml_dtypes
import numpy as np
from jax import lax
from jax.experimental import pallas as pl
from jax.experimental.pallas import tpu as pltpu
from jax.sharding import PartitionSpec as P

BINS = 96
HOP = 256
HALO = 1024
KERNEL = 2304
TAPS = KERNEL // HOP
MARGIN = HALO // HOP
WATER = 0.1
EPSILON = 1e-06
MOST = 2
LANES = 128
MESH = pl.DeviceIdType.MESH


def cq_table():
    f32 = np.float32
    octave_bins = BINS // 8
    index = np.arange(BINS).astype(f32)
    freq = f32(0.25) * np.exp2(((index - f32(BINS - 1)) / f32(octave_bins)).astype(np.float64)).astype(f32)
    quality = f32(1.0 / (2.0 ** (1.0 / octave_bins) - 1.0))
    support = np.minimum(quality / freq, f32(KERNEL))
    offset = np.arange(KERNEL).astype(f32) - f32(0.5 * (KERNEL - 1))
    ratio = (offset[:, None] / support[None, :]).astype(np.float64)
    window = np.where(np.abs(ratio) < 0.5, 0.5 + 0.5 * np.cos(2.0 * math.pi * ratio), 0.0)
    window = window / np.sqrt(np.sum(window * window, axis=0, keepdims=True))
    cycles = offset[:, None] * freq[None, :]
    phase = (cycles - np.floor(cycles)).astype(np.float64)
    table = np.zeros((KERNEL, 2 * LANES))
    table[:, :BINS] = window * np.cos(2.0 * math.pi * phase)
    table[:, LANES : LANES + BINS] = -window * np.sin(2.0 * math.pi * phase)
    return table.astype(f32).astype(ml_dtypes.bfloat16)


def ring_rows(chips, rec_dev):
    half = chips // 2
    return [min(rec_dev, 2 * MOST * (half - k) + MOST) for k in range(1, half + 1)]


def ring_groups(hops):
    depth = [sum(n > p for n in hops) for p in range(hops[0])]
    firsts = [p for p in range(len(depth)) if p == 0 or depth[p] != depth[p - 1]] + [len(depth)]
    return [(a, b - a, depth[a]) for a, b in zip(firsts[:-1], firsts[1:])]


def kernel(
    sizes, rec_in, owner, valid, mask, table_in, out, table, bins, across,
    ext, coef, adj, acc, lv_out, lv_in, meta_out, meta_in, order, meta_s, order_s,
    flat, rows, packet, mate_out, mate_in, slots,
    halo_send, halo_recv, one_send, one_recv, ring_send, ring_recv, mate_recv, local, *bufs,
):
    chips, groups, comps, rec_dev, frames = sizes
    half = chips // 2
    traces = comps * rec_dev
    per_row = frames * HOP // LANES
    hops = ring_rows(chips, rec_dev)
    parts = ring_groups(hops)
    samples = frames * HOP
    f32, i32 = jnp.float32, jnp.int32

    space, t = lax.axis_index("space"), lax.axis_index("tm")
    z, core = space // 2, space % 2

    def band(d):
        return {"tm": lax.rem(t + d + groups, groups)}

    def chip(d):
        return {"space": lax.rem(z + d + chips, chips) * 2 + core}

    mate = {"space": z * 2 + 1 - core}

    def send(src, dst, ss, rs, to):
        copy = pltpu.make_async_remote_copy(src, dst, ss, rs, device_id=to, device_id_type=MESH)
        copy.start()
        return copy

    def wait_bytes(ref, sem):
        pltpu.make_async_copy(ref, ref, sem).wait()

    barrier = pltpu.get_barrier_semaphore()
    others = [band(d) for d in range(1, groups)] + [chip(d) for d in range(1, chips)] + [mate]
    for to in others:
        pl.semaphore_signal(barrier, inc=1, device_id=to, device_id_type=MESH)

    rec_copy = pltpu.make_async_copy(rec_in, ext.at[:, :, :, pl.ds(2 * HALO, samples)], local.at[3])
    rec_copy.start()
    table_copy = pltpu.make_async_copy(table_in, table, local.at[4])
    table_copy.start()

    pl.semaphore_wait(barrier, len(others))

    halo = {}
    after = 2 * HALO + samples
    for part, s in ((0, 1), (0, 0), (1, 1), (1, 0)):
        for side in range(2):
            at, to = [
                [(samples - HALO, HALO), (samples - 2 * HALO, 0)],
                [(0, after), (HALO, after + HALO)],
            ][side][part]
            n = (part * 2 + s) * 2 + side
            halo[part, s, side] = send(
                rec_in.at[s, :, :, pl.ds(at, HALO)], ext.at[s, :, :, pl.ds(to, HALO)],
                halo_send.at[n], halo_recv.at[n], band(1 - 2 * side),
            )

    def analyse(s, first_f, number):
        blocks = [
            jnp.concatenate([ext[s, c, :, pl.ds((first_f + b) * HOP, HOP)] for c in range(comps)], axis=0)
            for b in range(number + 2 * MARGIN)
        ]
        total = None
        for tap in range(TAPS):
            term = jnp.dot(
                jnp.concatenate(blocks[tap : tap + number], axis=0),
                table[pl.ds(tap * HOP, HOP), :],
                preferred_element_type=f32,
            )
            total = term if total is None else total + term
        coef[s, pl.ds(first_f * traces, number * traces), :] = total.astype(jnp.bfloat16)

    def take_halo(part, s):
        halo[part, s, 0].wait_recv()
        halo[part, s, 1].wait_recv()
        low = (1 - part) * HALO

        @pl.when(t == 0)
        def _():
            ext[s, :, :, pl.ds(low, HALO)] = jnp.zeros((comps, rec_dev, HALO), jnp.bfloat16)

        @pl.when(t == groups - 1)
        def _():
            ext[s, :, :, pl.ds(after + part * HALO, HALO)] = jnp.zeros((comps, rec_dev, HALO), jnp.bfloat16)

    table_copy.wait()
    rec_copy.wait()
    take_halo(0, 1)
    analyse(1, MARGIN, frames)
    diagonal = lax.broadcasted_iota(i32, (traces, LANES), 0) == lax.broadcasted_iota(i32, (traces, LANES), 1)
    power = jnp.zeros((traces, LANES), f32)
    for f in range(frames):
        o = coef[1, pl.ds((MARGIN + f) * traces, traces), :].astype(f32)
        power = power + (o[:, :LANES] * o[:, :LANES] + o[:, LANES:] * o[:, LANES:])
    power = jnp.broadcast_to(jnp.sum(power, axis=1, keepdims=True), (traces, LANES))
    power = jnp.sum(jnp.where(diagonal, power, 0.0), axis=0, keepdims=True)
    lv_out[...] = jnp.broadcast_to(power, lv_out.shape)
    for d in range(1, groups):
        send(lv_out, lv_in.at[d - 1], one_send.at[1], one_recv.at[1], band(d))
    lane = lax.broadcasted_iota(i32, (rec_dev, LANES), 1)
    line = lax.broadcasted_iota(i32, (rec_dev, LANES), 0)
    listed = lane < rec_dev

    def widened(ref, n):
        across[n : n + 1, pl.ds(0, rec_dev)] = ref[n : n + 1, :]
        return jnp.broadcast_to(across[n : n + 1, :], (rec_dev, LANES))

    def upright(values):
        return jnp.broadcast_to(jnp.sum(jnp.where(line == lane, values, 0), axis=1, keepdims=True), (rec_dev, LANES))

    across[...] = jnp.zeros_like(across)
    own_t = widened(owner, 0)
    own = upright(own_t)
    first, last = upright(widened(valid, 0)), upright(widened(valid, 1))
    bins[...] = jnp.zeros_like(bins)
    bins[:, pl.ds(0, BINS)] = mask[...].astype(f32)
    before = listed & (lane < line)

    def count(what):
        return jnp.broadcast_to(jnp.sum(jnp.where(what, 1, 0), axis=1, keepdims=True), (rec_dev, LANES))

    def count_t(what):
        return jnp.broadcast_to(jnp.sum(jnp.where(what, 1, 0), axis=0, keepdims=True), (rec_dev, LANES))

    far = lax.rem(own // 2 + chips - z, chips)
    far_t = lax.rem(own_t // 2 + chips - z, chips)
    rank = count(before & (own_t == own))
    turn = count(before & (far_t == half))
    turn_t = count_t((line < lane) & (far == half))
    up = ((far > 0) & (far < half)) | ((far == half) & (turn % 2 == 0))
    up_t = ((far_t > 0) & (far_t < half)) | ((far_t == half) & (turn_t % 2 == 0))
    down = (far > half) | ((far == half) & (turn % 2 == 1))
    down_t = (far_t > half) | ((far_t == half) & (turn_t % 2 == 1))
    same = before & (far_t == far)
    place_up = count(listed & up_t & ((far_t > far) | same))
    place_down = count(listed & down_t & ((far_t < far) | same))
    place = jnp.where(up, place_up, jnp.where(down, rec_dev + place_down, line))
    key = far * (2 * MOST) + (own % 2) * MOST + rank
    sent = jnp.sum(jnp.where(key == lane, place + 1, 0), axis=0, keepdims=True)
    meta_out[...] = jnp.broadcast_to(sent, meta_out.shape)
    taken = jnp.sum(jnp.where((place == lane) & (up | down), line, 0), axis=0, keepdims=True)
    order[...] = jnp.broadcast_to(taken, order.shape)
    order_copy = pltpu.make_async_copy(order, order_s, local.at[0])
    order_copy.start()
    own_copy = pltpu.make_async_copy(meta_out, meta_s.at[0], local.at[1])
    own_copy.start()
    for d in range(1, chips):
        send(meta_out, meta_in.at[d - 1], one_send.at[0], one_recv.at[0], chip(d))

    take_halo(0, 0)
    analyse(0, MARGIN, frames)
    for s in (1, 0):
        take_halo(1, s)
        analyse(s, 0, MARGIN)
        analyse(s, MARGIN + frames, MARGIN)

    wait_bytes(lv_in, one_recv.at[1])
    power = lv_out[...]
    for d in range(1, groups):
        power = power + lv_in[d - 1]
    power = jnp.broadcast_to(power[0:1], (traces, LANES))
    power = jnp.sum(jnp.where(diagonal, power, 0.0), axis=1, keepdims=True)
    level = jnp.broadcast_to(WATER * (power / (frames * groups * BINS)) + EPSILON, (traces, LANES))

    first, last, bands = (jnp.concatenate([v] * comps, axis=0) for v in (first, last, bins[...]))
    for f in range(frames + 2 * MARGIN):
        center = (t * frames + f - MARGIN) * HOP + HOP // 2
        weight = jnp.where((first <= center) & (center < last), bands, 0.0)
        x = coef[0, pl.ds(f * traces, traces), :].astype(f32)
        y = coef[1, pl.ds(f * traces, traces), :].astype(f32)
        x_re, x_im, y_re, y_im = x[:, :LANES], x[:, LANES:], y[:, :LANES], y[:, LANES:]
        x_inv = lax.rsqrt(x_re * x_re + x_im * x_im + level)
        y_inv = lax.rsqrt(y_re * y_re + y_im * y_im + level)
        d_re = weight * (x_re * x_inv - y_re * y_inv)
        d_im = weight * (x_im * x_inv - y_im * y_inv)
        inner = (x_re * d_re + x_im * d_im) * (x_inv * x_inv * x_inv)
        adj[pl.ds(f * traces, traces), pl.ds(0, LANES)] = (d_re * x_inv - x_re * inner).astype(jnp.bfloat16)
        adj[pl.ds(f * traces, traces), pl.ds(LANES, LANES)] = (d_im * x_inv - x_im * inner).astype(jnp.bfloat16)

    for tap in range(TAPS):
        term = lax.dot_general(
            adj[pl.ds((2 * MARGIN - tap) * traces, frames * traces), :], table[pl.ds(tap * HOP, HOP), :],
            (((1,), (1,)), ((), ())), preferred_element_type=f32,
        )
        acc[...] = term if tap == 0 else acc[...] + term
    for b in range(frames):
        block = acc[pl.ds(b * traces, traces), :]
        for h in range(HOP // LANES):
            j = b * (HOP // LANES) + h
            flat[pl.ds(j * traces, traces), :] = block[:, h * LANES : (h + 1) * LANES]

    order_copy.wait()
    own_copy.wait()
    for c in range(comps):
        for r in range(rec_dev):
            row = flat[pl.ds(c * rec_dev + r, per_row, stride=traces), :]
            rows[r, pl.ds(c * per_row, per_row), :] = row.astype(jnp.bfloat16)
    flying = {}

    def hop(k, g, i):
        first_p, number, _ = parts[g]
        run = pl.ds(first_p, number)
        src = packet.at[i, run] if k == 1 else bufs[2 * (k - 2) + i].at[run]
        if k > 2:
            flying[k - 2, g, i].wait_send()
        flying[k, g, i] = send(
            src, bufs[2 * (k - 1) + i].at[run], ring_send.at[(g * 2 + k % 2) * 2 + i],
            ring_recv.at[((k - 1) * len(parts) + g) * 2 + i], chip(1 - 2 * i),
        )

    for g, (first_p, number, _) in enumerate(parts):
        for i in range(2):
            for p in range(first_p, first_p + number):
                packet[i, p] = rows[order_s[0, i * rec_dev + p]]
            hop(1, g, i)

    wait_bytes(meta_in, one_recv.at[0])
    got = pltpu.make_async_copy(meta_in, meta_s.at[pl.ds(1, chips - 1)], local.at[2])
    got.start()
    got.wait()

    whole = comps * per_row

    def keep(source, rank, row, whose):
        slot = (lax.rem(z + source + chips, chips) * 2 + whose) * MOST + rank
        slots[pl.ds(pl.multiple_of(slot * whole, whole), whole), :] = row.astype(f32)

    def deal(source, j, read):
        for e in range(2 * MOST):
            mine, rank = e // MOST == 0, e % MOST
            whose = core if mine else 1 - core
            away = (-source) % chips
            v = meta_s[away, 0, away * 2 * MOST + whose * MOST + rank]
            row = jnp.where(v > 0, read(v), jnp.zeros((), jnp.bfloat16))
            if mine:
                keep(source, rank, row, core)
            else:
                mate_out[j, rank] = row

    def from_ring(k, i):
        def read(v):
            at = jnp.clip(v - 1 - i * rec_dev, 0, hops[k - 1] - 1)
            return bufs[2 * (k - 1) + i][at]

        return read

    def from_both(v):
        return jnp.where(v > rec_dev, from_ring(half, 1)(v), from_ring(half, 0)(v))

    deal(0, 0, lambda v: rows[jnp.clip(v - 1, 0, rec_dev - 1)])
    mates = []

    def to_mate(first_j, number):
        ref = (mate_out.at[pl.ds(first_j, number)], mate_in.at[pl.ds(first_j, number)])
        mates.append((first_j, number, send(*ref, one_send.at[2], mate_recv.at[len(mates)], mate)))

    steps = sorted((k / (depth + 2), g, k) for g, (_, _, depth) in enumerate(parts) for k in range(1, depth + 1))
    waits = {k: sum(depth >= k for _, _, depth in parts) for k in range(1, half + 1)}
    ready = 1
    for _, g, k in steps:
        for i in range(2):
            flying[k, g, i].wait_recv()
            if k < parts[g][2]:
                hop(k + 1, g, i)
        waits[k] -= 1
        while ready < half and waits[ready] == 0:
            for i in range(2):
                deal(-ready if i == 0 else ready, 2 * ready - 1 + i, from_ring(ready, i))
            if ready % 2 == 1 and ready > 1:
                to_mate(*((0, 7) if ready == 3 else (2 * ready - 3, 4)))
            ready += 1
    deal(half, 2 * half - 1, from_both)
    to_mate(2 * half - 1, 1)
    source_of = [0] + [s for k in range(1, half) for s in (-k, k)] + [half]
    for first_j, number, copy in mates:
        copy.wait_recv()
        for j in range(first_j, first_j + number):
            for rank in range(MOST):
                keep(source_of[j], rank, mate_in[j, rank], 1 - core)
    kept = chips * 2 * MOST
    for c in range(comps):
        for j in range(per_row):
            part = slots[pl.ds(c * per_row + j, kept, stride=whole), :]
            out[c, :, pl.ds(j * LANES, LANES)] = part.astype(jnp.bfloat16)

    for copy in halo.values():
        copy.wait_send()
    for g, (_, _, depth) in enumerate(parts):
        for k in range(max(1, depth - 1), depth + 1):
            for i in range(2):
                flying[k, g, i].wait_send()
    wait_bytes(meta_in, one_send.at[0])
    wait_bytes(lv_in, one_send.at[1])
    wait_bytes(mate_out, one_send.at[2])


def solution(mesh):
    chips, groups = mesh.shape["space"] // 2, mesh.shape["tm"]

    def on_device(recordings, owner, valid_range, bin_mask):
        _, comps, rec_dev, samples = recordings.shape
        frames = samples // HOP
        traces, per_row = comps * rec_dev, samples // LANES
        kept = chips * 2 * MOST
        hops = ring_rows(chips, rec_dev)
        parts = len(ring_groups(hops))
        bf16, f32, i32 = jnp.bfloat16, jnp.float32, jnp.int32
        sizes = (chips, groups, comps, rec_dev, frames)
        dma = pltpu.SemaphoreType.DMA
        return pl.pallas_call(
            functools.partial(kernel, sizes),
            out_shape=jax.ShapeDtypeStruct((comps, kept, samples), bf16),
            in_specs=[pl.BlockSpec(memory_space=space) for space in (pl.ANY, pltpu.VMEM, pltpu.VMEM, pltpu.VMEM, pl.ANY)],
            out_specs=pl.BlockSpec(memory_space=pltpu.VMEM),
            scratch_shapes=[
                pltpu.VMEM((KERNEL, 2 * LANES), bf16),
                pltpu.VMEM((rec_dev, LANES), f32),
                pltpu.VMEM((8, LANES), i32),
                pltpu.VMEM((2, comps, rec_dev, samples + 4 * HALO), bf16),
                pltpu.VMEM((2, (frames + 2 * MARGIN) * traces, 2 * LANES), bf16),
                pltpu.VMEM(((frames + 2 * MARGIN) * traces, 2 * LANES), bf16),
                pltpu.VMEM((frames * traces, HOP), f32),
                pltpu.VMEM((8, LANES), f32),
                pltpu.VMEM((groups - 1, 8, LANES), f32),
                pltpu.VMEM((8, LANES), i32),
                pltpu.VMEM((chips - 1, 8, LANES), i32),
                pltpu.VMEM((8, LANES), i32),
                pltpu.SMEM((chips, 8, LANES), i32),
                pltpu.SMEM((8, LANES), i32),
                pltpu.VMEM((per_row * traces, LANES), f32),
                pltpu.VMEM((rec_dev, comps * per_row, LANES), bf16),
                pltpu.VMEM((2, rec_dev, comps * per_row, LANES), bf16),
                pltpu.VMEM((chips, MOST, comps * per_row, LANES), bf16),
                pltpu.VMEM((chips, MOST, comps * per_row, LANES), bf16),
                pltpu.VMEM((kept * comps * per_row, LANES), f32),
                dma((8,)), dma((8,)), dma((3,)), dma((2,)),
                dma((4 * parts,)), dma((chips * parts,)), dma((chips // 4,)), dma((5,)),
            ] + [pltpu.VMEM((n, comps * per_row, LANES), bf16) for n in hops for _ in range(2)],
            compiler_params=pltpu.CompilerParams(
                collective_id=0, has_side_effects=True, vmem_limit_bytes=60 << 20
            ),
        )(recordings, owner.T, valid_range.T, bin_mask, jnp.asarray(cq_table()))

    return jax.shard_map(
        on_device,
        mesh=mesh,
        in_specs=(
            P(None, None, "space", "tm"),
            P("space", None),
            P("space", None),
            P("space", None),
        ),
        out_specs=P(None, "space", "tm"),
        check_vma=False,
    )
```

time: 75.3 us -> 67.3 us (0.89)
  Pallas kernels: 73 us -> 65 us
    pallas_call x1, Pallas kernels: 73 us -> 65 us  [on_device(): pl.pallas_call(functools.partial(kernel, sizes), out_shape=jax.ShapeDtype...]
where the time goes in v4:
time: 67.3 us; the launch traced here: 67.1 us
  Pallas kernels  65 us (97%)
  local copies, waits for them, and re-layouts  2.09 us (3%)
    pallas_call x1, Pallas kernels, on_device(): pl.pallas_call(functools.partial(kernel, sizes), out_shape=jax.ShapeDtype...  65 us
    unnamed x1, local copies, waits for them, and re-layouts  2.09 us

profile of v4, /device:TPU:1, one launch (start us, length us, event | category | flops | bytes accessed | tf_op | source)
XLA Modules:
  0.0 67.1 jit_solution(8680847279513490893)
XLA Ops:
  0.0 65.0 %shard_map.55 = bf16[3,64,2048]{2,1,0:T(8,128)(2,1)} custom-call(bf16[2,3,16,2048]{3,2,1,0:T(8,128)(2,1)} %rec_in.1, s32[1,16]{1,0:T(1,128)} %bitcast.3, s32[2,16]{1,0:T(2,128)} %bitcast.2, s32[16,96]{1,0:T(8,128)} %mask.1, bf16[2304,256]{1,0:T(8,128)(2,1)} %constant.2.clone.table_in), custom_call_target="tpu_custom_call" | custom-call | tf_op jit(solution)/shard_map/pallas_call | solution.py:368
  65.0 2.1 %copy.7 = bf16[3,64,2048]{2,1,0:T(8,128)(2,1)} copy(bf16[3,64,2048]{2,1,0:T(8,128)(2,1)} %shard_map.55) | data formatting | bytes 1572864

commit v5 on v4

--- a/solution.py
+++ b/solution.py
@@ -365,9 +365,11 @@
         bf16, f32, i32 = jnp.bfloat16, jnp.float32, jnp.int32
         sizes = (chips, groups, comps, rec_dev, frames)
         dma = pltpu.SemaphoreType.DMA
+        args = (recordings, owner.T, valid_range.T, bin_mask, jnp.asarray(cq_table()))
+        args = [pltpu.with_memory_space_constraint(x, pltpu.HBM) for x in args]
         return pl.pallas_call(
             functools.partial(kernel, sizes),
-            out_shape=jax.ShapeDtypeStruct((comps, kept, samples), bf16),
+            out_shape=pltpu.VMEM((comps, kept, samples), bf16),
             in_specs=[pl.BlockSpec(memory_space=space) for space in (pl.ANY, pltpu.VMEM, pltpu.VMEM, pltpu.VMEM, pl.ANY)],
             out_specs=pl.BlockSpec(memory_space=pltpu.VMEM),
             scratch_shapes=[
@@ -395,9 +397,9 @@
                 dma((4 * parts,)), dma((chips * parts,)), dma((chips // 4,)), dma((5,)),
             ] + [pltpu.VMEM((n, comps * per_row, LANES), bf16) for n in hops for _ in range(2)],
             compiler_params=pltpu.CompilerParams(
-                collective_id=0, has_side_effects=True, vmem_limit_bytes=60 << 20
+                collective_id=0, has_side_effects=True, vmem_limit_bytes=40 << 20
             ),
-        )(recordings, owner.T, valid_range.T, bin_mask, jnp.asarray(cq_table()))
+        )(*args)
 
     return jax.shard_map(
         on_device,

time: 67.3 us -> 65.2 us (0.969)
  local copies, waits for them, and re-layouts: 2.09 us -> 0.88 us
  Pallas kernels: 65 us -> 64.2 us
    unnamed x1, local copies, waits for them, and re-layouts: 2.09 us -> 0.88 us
    pallas_call x1, Pallas kernels: 65 us -> 64.2 us  [on_device(): pl.pallas_call(functools.partial(kernel, sizes), out_shape=pltpu.VMEM((co...]
where the time goes in v5:
time: 65.2 us; the launch traced here: 65.1 us
  Pallas kernels  64.2 us (98%)
  local copies, waits for them, and re-layouts  0.88 us (1%)
    pallas_call x1, Pallas kernels, on_device(): pl.pallas_call(functools.partial(kernel, sizes), out_shape=pltpu.VMEM((co...  64.2 us

profile of v5, /device:TPU:1, one launch (start us, length us, event | category | flops | bytes accessed | tf_op | source)
XLA Modules:
  0.0 65.1 jit_solution(9856226887067350266)
XLA Ops:
  0.0 64.2 %shard_map.55 = bf16[3,64,2048]{2,1,0:T(8,128)(2,1)S(1)} custom-call(bf16[2,3,16,2048]{3,2,1,0:T(8,128)(2,1)} %rec_in.1, s32[1,16]{1,0:T(1,128)} %bitcast.3, s32[2,16]{1,0:T(2,128)} %bitcast.2, s32[16,96]{1,0:T(8,128)} %mask.1, bf16[2304,256]{1,0:T(8,128)(2,1)} %constant.2.clone.table_in), custom_call_target="tpu_custom_call" | custom-call | tf_op jit(solution)/shard_map/pallas_call | solution.py:370
  64.2 0.9 %copy.7 = bf16[3,64,2048]{2,1,0:T(8,128)(2,1)} copy(bf16[3,64,2048]{2,1,0:T(8,128)(2,1)S(1)} %shard_map.55) | data formatting | bytes 1572864
